TPU v7x, 512 devices: a whole 4x8x8 slice. The times are simulated.
512 devices in a mesh: batch: 32 (over z, x), blk: 16 (over y, core).
Axes of the slice: x: 4, y: 8, z: 8, core: 2. Of those that a mesh axis runs over, the one named last changes fastest.
Arguments:
- points: float32 [1024, 16, 3, 256], P('batch', 'blk'), may hold values from -6 to 6
- centers: float32 [1024, 16, 3, 384], P('batch', 'blk'), may hold values from -6 to 6
- exponents: float32 [1024, 16, 384], P('batch', 'blk'), may hold values from 0.1 to 1
- angular: float32 [1024, 16, 3, 384], P('batch', 'blk'), may hold values from -3 to 3
- grid_weights: float32 [1024, 16, 256], P('batch', 'blk'), may hold values from 0.001 to 0.01
- hartree: float32 [1024, 16, 256], P('batch', 'blk'), may hold values from 0 to 1.7
- load_plan: int32 [16, 1024], P('blk'), may hold values from 0 to 1023, each once within a row
- density_blocks: bfloat16 [256, 128, 128], P('blk'), may hold values from -0.046875 to 0.046875
- pair_lists: int32 [32, 16, 16, 2], P('batch', 'blk'), may hold values from 0 to 15
- batch_pairs: int32 [1024, 16, 9], P('batch', 'blk'), may hold values from 0 to 31, as said below
Outputs:
- hamiltonian: float32 [256, 128, 128], P('blk')
- density: float32 [1024, 16, 256], P('batch', 'blk')
Inputs may be any that keep to these rules, and one draw needn't show every extreme that they name: Each row of load_plan names every storage row of its column once. `pair_lists`: local index of a block pair within the 16 pairs held by one index of blk. `batch_pairs`: entry e of a device's table is the (e % 2)-th block it reads from index e // 2 of blk; every entry of a device's table is named by some pair of its batches.
All inputs are finite; a program needn't handle non-finite values.
Results may differ from a plain program's by a relative error of at most 0.0065.
Values may be sent and summed in bfloat16 or wider, within the bound.
No kernel may reach another device: no remote copies, remote signals or barrier semaphores. Data moves between devices by JAX's collectives and lax.ppermute only.
A program may use at most 64 MiB of HBM per device.

v0:
```python
import jax
import jax.numpy as jnp
from jax import lax
from jax.sharding import PartitionSpec as P

LIST = 3
xc_scale = 0.98474502
soft_square = 0.01


def exchange_potential(grid_rho):
    return -xc_scale * jnp.power(grid_rho * grid_rho + soft_square, 1.0 / 6.0)


def evaluate(points, centers, exponents, angular):
    distance = jnp.zeros(points.shape[:-2] + (points.shape[-1], centers.shape[-1]), jnp.float32)
    angular_part = jnp.ones_like(distance)
    for component in range(3):
        delta = points[..., component, :, None] - centers[..., component, None, :]
        distance = distance + delta * delta
        angular_part = angular_part + angular[..., component, None, :] * delta
    return (jnp.exp(-exponents[..., None, :] * distance) * angular_part).astype(jnp.bfloat16)


def on_device(
    points,
    centers,
    exponents,
    angular,
    grid_weights,
    hartree,
    load_plan,
    density_blocks,
    pair_lists,
    batch_pairs,
):
    slot_count = points.shape[0]
    grid_size = points.shape[3]
    columns = lax.axis_size("blk")
    per_owner = pair_lists.shape[3]
    held_pairs = density_blocks.shape[0]
    block_size = density_blocks.shape[1]
    entries = columns * per_owner
    list_size = LIST
    basis_width = list_size * block_size
    batch_rank = lax.axis_index("batch")
    plan_rows = lax.dynamic_slice_in_dim(load_plan[0], batch_rank * slot_count, slot_count)
    stored = lax.all_gather(hartree[:, 0, :], "batch", axis=0, tiled=True)
    potential = stored[plan_rows]
    wanted = pair_lists[0, 0]
    asked_slots = lax.all_to_all(wanted, "blk", split_axis=0, concat_axis=0, tiled=True)
    owner_base = jnp.arange(entries, dtype=jnp.int32) // per_owner * held_pairs
    global_ids = owner_base + wanted.reshape(entries)
    blank_table = jnp.zeros((entries, block_size, block_size), jnp.bfloat16)
    piece = lax.all_gather(density_blocks, "blk", axis=0, tiled=True)
    inside = (global_ids >= 0) & (global_ids < piece.shape[0])
    chosen = piece[jnp.clip(global_ids, 0, piece.shape[0] - 1)]
    fetched = jnp.where(inside[:, None, None], chosen, blank_table)
    group_size = 4
    loop_turns = slot_count // group_size

    def take_rows(value, turn_index):
        return lax.dynamic_slice_in_dim(value, turn_index * group_size, group_size, 0)

    def integrate(partial_table, turn_index):
        basis = evaluate(
            take_rows(points, turn_index)[:, 0],
            take_rows(centers, turn_index)[:, 0],
            take_rows(exponents, turn_index)[:, 0],
            take_rows(angular, turn_index)[:, 0],
        )
        slot_refs = take_rows(batch_pairs, turn_index)[:, 0]
        blocks = fetched[slot_refs]
        sub_density = (
            blocks.reshape(group_size, list_size, list_size, block_size, block_size)
            .transpose(0, 1, 3, 2, 4)
            .reshape(group_size, basis_width, basis_width)
        )
        inner = jnp.einsum("gpm,gmn->gpn", basis, sub_density, preferred_element_type=jnp.float32)
        grid_rho = jnp.sum(inner * basis.astype(jnp.float32), axis=-1)
        effective = take_rows(potential, turn_index) + exchange_potential(grid_rho)
        weight_rows = take_rows(grid_weights, turn_index)[:, 0]
        scaled = ((weight_rows * effective)[..., None] * basis.astype(jnp.float32)).astype(
            jnp.bfloat16
        )
        full_blocks = jnp.einsum("gpm,gpn->gmn", basis, scaled, preferred_element_type=jnp.float32)
        contributions = (
            full_blocks.reshape(group_size, list_size, block_size, list_size, block_size)
            .transpose(0, 1, 3, 2, 4)
            .reshape(group_size * list_size * list_size, block_size, block_size)
        )
        partial_table = partial_table.at[slot_refs.reshape(-1)].add(contributions)
        return (partial_table, grid_rho)

    zero_table = jnp.zeros((entries, block_size, block_size), jnp.float32)
    partial_table, rho_groups = lax.scan(integrate, zero_table, jnp.arange(loop_turns))
    grid_rho = rho_groups.reshape(slot_count, grid_size)
    received = lax.all_to_all(
        partial_table.reshape(columns, per_owner, block_size, block_size),
        "blk",
        split_axis=0,
        concat_axis=0,
        tiled=True,
    )
    owned_sums = (
        jnp.zeros((held_pairs, block_size, block_size), jnp.float32)
        .at[asked_slots.reshape(entries)]
        .add(received.reshape(entries, block_size, block_size))
    )
    hamiltonian = lax.psum(owned_sums, "batch")
    batch_total = load_plan.shape[1]
    placement = (plan_rows[None, :] == jnp.arange(batch_total, dtype=jnp.int32)[:, None]).astype(
        jnp.float32
    )
    spread_rows = jnp.dot(
        placement, grid_rho, precision=lax.Precision.HIGHEST, preferred_element_type=jnp.float32
    )
    density = lax.psum_scatter(spread_rows, "batch", scatter_dimension=0, tiled=True)
    return (hamiltonian, density[:, None, :])


def solution(mesh):
    return jax.shard_map(
        on_device,
        mesh=mesh,
        in_specs=(
            P("batch", "blk", None, None),
            P("batch", "blk", None, None),
            P("batch", "blk", None),
            P("batch", "blk", None, None),
            P("batch", "blk", None),
            P("batch", "blk", None),
            P("blk", None),
            P("blk", None, None),
            P("batch", "blk", None, None),
            P("batch", "blk", None),
        ),
        out_specs=(P("blk", None, None), P("batch", "blk", None)),
        check_vma=False,
    )
```

profile of v0, /device:TPU:8, one launch (start us, length us, event | category | flops | bytes accessed | tf_op | source)
XLA Modules:
  0.0 800.7 jit_solution(2311108223574678586)
XLA Ops:
  10.7 9.1 %all-to-all-start = ((s32[16,1,2]{2,1,0:T(1,128)}), s32[16,1,2]{2,1,0:T(1,128)S(1)}, u32[]{:S(2)}, u32[]{:S(2)}) async-start(s32[16,1,2]{2,1,0:T(1,128)} %copy.56), calls=%async_computation | async-start | bytes 16384 | tf_op jit(solution)/shard_map/all_to_all | solution.py:51
  22.3 76.3 %all-gather.6.cloned.1.call-done = f32[1024,1,256]{2,0,1:T(8,128)} async-done(((f32[32,1,256]{2,0,1:T(8,128)}), f32[1024,1,256]{2,0,1:T(8,128)}) %all-gather.6.cloned.1.call-update) | async-done | bytes 1048592 | tf_op jit(solution)/shard_map/all_gather | solution.py:48
  100.4 54.4 %all-gather.4.cloned.1.call-done = bf16[256,128,128]{2,1,0:T(8,128)(2,1)} async-done(((bf16[16,128,128]{2,1,0:T(8,128)(2,1)}), bf16[256,128,128]{2,1,0:T(8,128)(2,1)}) %all-gather.4.cloned.1.call-update) | async-done | bytes 8388624 | tf_op jit(solution)/shard_map/all_gather | solution.py:55
  154.8 4.1 gather_fusion.2
  160.6 234.9 %while.12 = (s32[]{:T(128)}, f32[32,128,128]{2,1,0:T(8,128)}, f32[8,4,256]{2,1,0:T(4,128)S(1)}, s32[8]{0:T(128)S(1)}, s32[32,1,9]{2,0,1:T(8,128)S(1)}, /*index=5...) while((s32[]{:T(128)}, f32[32,128,128]{2,1,0:T(8,128)}, ...), condition=%wide.region_3.4_spmd, body=%wide.region_0.3_spmd.sunk | while | flops 633674496 | bytes 35997664 | solution.py:96
  170.8 4.2 fusion.51
  175.1 3.5 reshape.302
  180.3 9.6 %scatter_fusion = f32[32,128,128]{2,1,0:T(8,128)} fusion(f32[32,128,128]{2,1,0:T(8,128)} %get-tuple-element.276, s32[36]{0:T(128)S(1)} %fusion.47, f32[36,128,128]{2,1,0:T(8,128)} %bitcast.106), kind=kCustom, calls=%fused_computation.3.clone.1 | custom fusion | flops 589824 | bytes 7078032 | tf_op jit(solution)/shard_map/while/body/eval_jaxpr/scatter-add | solution.py:92
  200.2 4.2 fusion.51
  204.4 3.5 reshape.302
  209.7 9.7 %scatter_fusion = f32[32,128,128]{2,1,0:T(8,128)} fusion(f32[32,128,128]{2,1,0:T(8,128)} %get-tuple-element.276, s32[36]{0:T(128)S(1)} %fusion.47, f32[36,128,128]{2,1,0:T(8,128)} %bitcast.106), kind=kCustom, calls=%fused_computation.3.clone.1 | custom fusion | flops 589824 | bytes 7078032 | tf_op jit(solution)/shard_map/while/body/eval_jaxpr/scatter-add | solution.py:92
  229.6 4.2 fusion.51
  233.8 3.5 reshape.302
  239.1 9.7 %scatter_fusion = f32[32,128,128]{2,1,0:T(8,128)} fusion(f32[32,128,128]{2,1,0:T(8,128)} %get-tuple-element.276, s32[36]{0:T(128)S(1)} %fusion.47, f32[36,128,128]{2,1,0:T(8,128)} %bitcast.106), kind=kCustom, calls=%fused_computation.3.clone.1 | custom fusion | flops 589824 | bytes 7078032 | tf_op jit(solution)/shard_map/while/body/eval_jaxpr/scatter-add | solution.py:92
  259.0 4.2 fusion.51
  263.2 3.5 reshape.302
  268.5 9.7 %scatter_fusion = f32[32,128,128]{2,1,0:T(8,128)} fusion(f32[32,128,128]{2,1,0:T(8,128)} %get-tuple-element.276, s32[36]{0:T(128)S(1)} %fusion.47, f32[36,128,128]{2,1,0:T(8,128)} %bitcast.106), kind=kCustom, calls=%fused_computation.3.clone.1 | custom fusion | flops 589824 | bytes 7078032 | tf_op jit(solution)/shard_map/while/body/eval_jaxpr/scatter-add | solution.py:92
  288.4 4.2 fusion.51
  292.6 3.5 reshape.302
  297.9 9.7 %scatter_fusion = f32[32,128,128]{2,1,0:T(8,128)} fusion(f32[32,128,128]{2,1,0:T(8,128)} %get-tuple-element.276, s32[36]{0:T(128)S(1)} %fusion.47, f32[36,128,128]{2,1,0:T(8,128)} %bitcast.106), kind=kCustom, calls=%fused_computation.3.clone.1 | custom fusion | flops 589824 | bytes 7078032 | tf_op jit(solution)/shard_map/while/body/eval_jaxpr/scatter-add | solution.py:92
  317.8 4.2 fusion.51
  322.0 3.5 reshape.302
  327.3 9.6 %scatter_fusion = f32[32,128,128]{2,1,0:T(8,128)} fusion(f32[32,128,128]{2,1,0:T(8,128)} %get-tuple-element.276, s32[36]{0:T(128)S(1)} %fusion.47, f32[36,128,128]{2,1,0:T(8,128)} %bitcast.106), kind=kCustom, calls=%fused_computation.3.clone.1 | custom fusion | flops 589824 | bytes 7078032 | tf_op jit(solution)/shard_map/while/body/eval_jaxpr/scatter-add | solution.py:92
  347.1 4.2 fusion.51
  356.6 9.6 %scatter_fusion = f32[32,128,128]{2,1,0:T(8,128)} fusion(f32[32,128,128]{2,1,0:T(8,128)} %get-tuple-element.276, s32[36]{0:T(128)S(1)} %fusion.47, f32[36,128,128]{2,1,0:T(8,128)} %bitcast.106), kind=kCustom, calls=%fused_computation.3.clone.1 | custom fusion | flops 589824 | bytes 7078032 | tf_op jit(solution)/shard_map/while/body/eval_jaxpr/scatter-add | solution.py:92
  376.5 4.2 fusion.51
  380.7 3.5 reshape.302
  386.0 9.6 %scatter_fusion = f32[32,128,128]{2,1,0:T(8,128)} fusion(f32[32,128,128]{2,1,0:T(8,128)} %get-tuple-element.276, s32[36]{0:T(128)S(1)} %fusion.47, f32[36,128,128]{2,1,0:T(8,128)} %bitcast.106), kind=kCustom, calls=%fused_computation.3.clone.1 | custom fusion | flops 589824 | bytes 7078032 | tf_op jit(solution)/shard_map/while/body/eval_jaxpr/scatter-add | solution.py:92
  395.5 6.8 all-to-all-start.1
  406.1 43.7 %all-to-all-done.1 = f32[16,2,128,128]{3,2,1,0:T(8,128)S(1)} async-done(((f32[16,2,128,128]{3,2,1,0:T(8,128)}), f32[16,2,128,128]{3,2,1,0:T(8,128)S(1)}, u32[]{:S(2)}, u32[]{:S(2)}) %all-to-all-start.1) | async-done | bytes 2097184 | tf_op jit(solution)/shard_map/all_to_all | solution.py:98
  453.5 175.6 %reduce-scatter.2.cloned.1.call-done = f32[32,256]{1,0:T(8,128)} async-done(((f32[1024,256]{1,0:T(8,128)}), f32[32,256]{1,0:T(8,128)}) %reduce-scatter.2.cloned.1.call-update) | async-done | bytes 32784 | tf_op jit(solution)/shard_map/reduce_scatter | solution.py:118
  630.5 161.3 %all-reduce.2.cloned.1.call-done = f32[16,128,128]{2,1,0:T(8,128)} async-done(((f32[16,128,128]{2,1,0:T(8,128)}), f32[16,128,128]{2,1,0:T(8,128)}) %all-reduce.2.cloned.1.call-update) | async-done | bytes 1048592 | tf_op jit(solution)/shard_map/psum | solution.py:110
  (263 shorter events, 114.2 us)
Async XLA Ops:
  7.2 91.4 %all-gather.6.cloned.1.call-start = ((), (), s32[]{:S(2)}) async-start(), calls=%async_computation.6 | async-start | bytes 1081344 | tf_op jit(solution)/shard_map/all_gather | solution.py:48
  8.6 146.2 %all-gather.4.cloned.1.call-start = ((), (), s32[]{:S(2)}) async-start(), calls=%async_computation.3 | async-start | bytes 8912896 | tf_op jit(solution)/shard_map/all_gather | solution.py:55
  10.7 384.8 %all-to-all-start = ((s32[16,1,2]{2,1,0:T(1,128)}), s32[16,1,2]{2,1,0:T(1,128)S(1)}, u32[]{:S(2)}, u32[]{:S(2)}) async-start(s32[16,1,2]{2,1,0:T(1,128)} %copy.56), calls=%async_computation | async-start | bytes 16384 | tf_op jit(solution)/shard_map/all_to_all | solution.py:51
  160.6 3.8 copy-start
  180.3 9.6 %copy-start.1 = (bf16[32,128,128]{2,1,0:T(8,128)(2,1)S(1)}, bf16[32,128,128]{2,1,0:T(8,128)(2,1)}, u32[]{:S(2)}) copy-start(bf16[32,128,128]{2,1,0:T(8,128)(2,1)} %copy-done) | copy-start | bytes 3145732 | tf_op jit(solution)/shard_map/while
  190.0 3.8 copy-start
  209.7 9.7 %copy-start.1 = (bf16[32,128,128]{2,1,0:T(8,128)(2,1)S(1)}, bf16[32,128,128]{2,1,0:T(8,128)(2,1)}, u32[]{:S(2)}) copy-start(bf16[32,128,128]{2,1,0:T(8,128)(2,1)} %copy-done) | copy-start | bytes 3145732 | tf_op jit(solution)/shard_map/while
  219.4 3.8 copy-start
  239.1 9.7 %copy-start.1 = (bf16[32,128,128]{2,1,0:T(8,128)(2,1)S(1)}, bf16[32,128,128]{2,1,0:T(8,128)(2,1)}, u32[]{:S(2)}) copy-start(bf16[32,128,128]{2,1,0:T(8,128)(2,1)} %copy-done) | copy-start | bytes 3145732 | tf_op jit(solution)/shard_map/while
  248.8 3.8 copy-start
  268.5 9.8 %copy-start.1 = (bf16[32,128,128]{2,1,0:T(8,128)(2,1)S(1)}, bf16[32,128,128]{2,1,0:T(8,128)(2,1)}, u32[]{:S(2)}) copy-start(bf16[32,128,128]{2,1,0:T(8,128)(2,1)} %copy-done) | copy-start | bytes 3145732 | tf_op jit(solution)/shard_map/while
  278.2 3.8 copy-start
  297.9 9.7 %copy-start.1 = (bf16[32,128,128]{2,1,0:T(8,128)(2,1)S(1)}, bf16[32,128,128]{2,1,0:T(8,128)(2,1)}, u32[]{:S(2)}) copy-start(bf16[32,128,128]{2,1,0:T(8,128)(2,1)} %copy-done) | copy-start | bytes 3145732 | tf_op jit(solution)/shard_map/while
  307.6 3.8 copy-start
  327.3 9.6 %copy-start.1 = (bf16[32,128,128]{2,1,0:T(8,128)(2,1)S(1)}, bf16[32,128,128]{2,1,0:T(8,128)(2,1)}, u32[]{:S(2)}) copy-start(bf16[32,128,128]{2,1,0:T(8,128)(2,1)} %copy-done) | copy-start | bytes 3145732 | tf_op jit(solution)/shard_map/while
  336.9 3.8 copy-start
  356.6 9.6 %copy-start.1 = (bf16[32,128,128]{2,1,0:T(8,128)(2,1)S(1)}, bf16[32,128,128]{2,1,0:T(8,128)(2,1)}, u32[]{:S(2)}) copy-start(bf16[32,128,128]{2,1,0:T(8,128)(2,1)} %copy-done) | copy-start | bytes 3145732 | tf_op jit(solution)/shard_map/while
  366.3 3.8 copy-start
  386.0 9.6 %copy-start.1 = (bf16[32,128,128]{2,1,0:T(8,128)(2,1)S(1)}, bf16[32,128,128]{2,1,0:T(8,128)(2,1)}, u32[]{:S(2)}) copy-start(bf16[32,128,128]{2,1,0:T(8,128)(2,1)} %copy-done) | copy-start | bytes 3145732 | tf_op jit(solution)/shard_map/while
  395.5 54.2 %all-to-all-start.1 = ((f32[16,2,128,128]{3,2,1,0:T(8,128)}), f32[16,2,128,128]{3,2,1,0:T(8,128)S(1)}, u32[]{:S(2)}, u32[]{:S(2)}) async-start(f32[16,2,128,128]{3,2,1,0:T(8,128)} %bitcast.108), calls=%async_computation.1 | async-start | bytes 4194304 | tf_op jit(solution)/shard_map/all_to_all | solution.py:98
  402.4 226.8 %reduce-scatter.2.cloned.1.call-start = ((), (), s32[]{:S(2)}) async-start(), calls=%async_computation.5 | async-start | bytes 1081344 | tf_op jit(solution)/shard_map/reduce_scatter | solution.py:118
  404.7 387.1 %all-reduce.2.cloned.1.call-start = ((), (), s32[]{:S(2)}) async-start(), calls=%async_computation.4 | async-start | bytes 2097152 | tf_op jit(solution)/shard_map/psum | solution.py:110
  452.5 1.0 copy-start.2
Sparse Core Ops, SparseCore 0:
  11.7 86.7 all-gather.5
  100.7 54.0 all-gather.3
  407.6 221.4 reduce-scatter.1
  633.0 158.7 all-reduce.1
where the time goes:
time: 804 us; the launch traced here: 801 us
  waiting for transfers between devices  512 us (64%)
  local copies, waits for them, and re-layouts  112 us (14%)
  other arithmetic  81.9 us (10%)
  matrix products  58.4 us (7%)
  starting transfers between devices  16.1 us (2%)
  between operations  13.9 us (2%)
    reduce_scatter x1, waiting for transfers between devices, on_device(): lax.psum_scatter(spread_rows, 'batch', scatter_dimension=0, tiled=True)  176 us
    psum x1, waiting for transfers between devices, on_device(): hamiltonian = lax.psum(owned_sums, 'batch')  161 us
    scatter-add x8, other arithmetic, integrate(): partial_table = partial_table.at[slot_refs.reshape(-1)].add(contributions)  77.2 us
    all_gather x1, waiting for transfers between devices, on_device(): stored = lax.all_gather(hartree[:, 0, :], 'batch', axis=0, tiled=True)  76.3 us
    all_gather x1, waiting for transfers between devices, on_device(): piece = lax.all_gather(density_blocks, 'blk', axis=0, tiled=True)  54.4 us
    all_to_all x1, waiting for transfers between devices, on_device(): lax.all_to_all(partial_table.reshape(columns, per_owner, block_size, bloc...  43.7 us
    dot_general x8, matrix products, integrate(): jnp.einsum('gpm,gpn->gmn', basis, scaled, preferred_element_type=jnp.floa...  33.7 us
    reshape x8, local copies, waits for them, and re-layouts, integrate(): full_blocks.reshape(group_size, list_size, block_size, list_size, block_s...  27.7 us
  transfers between devices with their start and end apart: 6, of which 5 were waited for; matrix products, arithmetic and copies ran while one was open for 31% of the time, Pallas kernels for 0%

commit v1 on v0

--- a/solution.py
+++ b/solution.py
@@ -6,6 +6,24 @@
 LIST = 3
 xc_scale = 0.98474502
 soft_square = 0.01
+
+
+def laid_out(blocks, dim):
+    dims = list(blocks.shape[1:])
+    dims[dim] *= blocks.shape[0]
+    return jnp.moveaxis(blocks, 0, dim).reshape(dims)
+
+
+def doubled(array, axis):
+    length = lax.axis_size(axis)
+    tiles = array[None]
+    for level in range(length.bit_length() - 1):
+        stride = 1 << level
+        partner_block = lax.ppermute(tiles, axis, [(i, i ^ stride) for i in range(length)])
+        both = jnp.stack([tiles, partner_block])
+        upper = lax.axis_index(axis) >> level & 1
+        tiles = jnp.where(upper == 0, both, both[::-1]).reshape(-1, *array.shape)
+    return tiles
 
 
 def exchange_potential(grid_rho):
@@ -45,7 +63,8 @@
     basis_width = list_size * block_size
     batch_rank = lax.axis_index("batch")
     plan_rows = lax.dynamic_slice_in_dim(load_plan[0], batch_rank * slot_count, slot_count)
-    stored = lax.all_gather(hartree[:, 0, :], "batch", axis=0, tiled=True)
+    value_2 = hartree[:, 0, :]
+    stored = laid_out(doubled(value_2, "batch"), 0)
     potential = stored[plan_rows]
     wanted = pair_lists[0, 0]
     asked_slots = lax.all_to_all(wanted, "blk", split_axis=0, concat_axis=0, tiled=True)

time: 804 us -> 728 us (0.905)
  waiting for transfers between devices: 512 us -> 413 us
  starting transfers between devices: 16.1 us -> 42.4 us
    all_gather x1 -> x0, waiting for transfers between devices: 76.3 us -> none  [on_device(): stored = lax.all_gather(hartree[:, 0, :], 'batch', axis=0, tiled=True)]
    all_gather x1, waiting for transfers between devices: 54.4 us -> 0.02 us  [on_device(): piece = lax.all_gather(density_blocks, 'blk', axis=0, tiled=True)]
    ppermute x0 -> x5, starting transfers between devices: none -> 27.4 us  [doubled(): lax.ppermute(tiles, axis, [(i, i ^ stride) for i in range(length)])]
    ppermute x0 -> x5, waiting for transfers between devices: none -> 26.5 us  [doubled(): lax.ppermute(tiles, axis, [(i, i ^ stride) for i in range(length)])]
  transfers between devices with their start and end apart: 6 -> 10, of which waited for: 5 -> 7; matrix products, arithmetic and copies ran while one was open for 31% -> 34% of each run, Pallas kernels for 0% -> 0%
where the time goes in v1:
time: 728 us; the launch traced here: 725 us
  waiting for transfers between devices  413 us (57%)
  local copies, waits for them, and re-layouts  109 us (15%)
  other arithmetic  82.6 us (11%)
  matrix products  58.2 us (8%)
  starting transfers between devices  42.4 us (6%)
  between operations  14 us (2%)
    reduce_scatter x1, waiting for transfers between devices, on_device(): lax.psum_scatter(spread_rows, 'batch', scatter_dimension=0, tiled=True)  181 us
    psum x1, waiting for transfers between devices, on_device(): hamiltonian = lax.psum(owned_sums, 'batch')  161 us
    scatter-add x8, other arithmetic, integrate(): partial_table = partial_table.at[slot_refs.reshape(-1)].add(contributions)  77.6 us
    all_to_all x1, waiting for transfers between devices, on_device(): lax.all_to_all(partial_table.reshape(columns, per_owner, block_size, bloc...  43.7 us
    dot_general x8, matrix products, integrate(): jnp.einsum('gpm,gpn->gmn', basis, scaled, preferred_element_type=jnp.floa...  33.5 us
    reshape x8, local copies, waits for them, and re-layouts, integrate(): full_blocks.reshape(group_size, list_size, block_size, list_size, block_s...  27.7 us
    ppermute x5, starting transfers between devices, doubled(): lax.ppermute(tiles, axis, [(i, i ^ stride) for i in range(length)])  27.4 us
    ppermute x5, waiting for transfers between devices, doubled(): lax.ppermute(tiles, axis, [(i, i ^ stride) for i in range(length)])  26.5 us
  transfers between devices with their start and end apart: 10, of which 7 were waited for; matrix products, arithmetic and copies ran while one was open for 34% of the time, Pallas kernels for 0%

profile of v1, /device:TPU:8, one launch (start us, length us, event | category | flops | bytes accessed | tf_op | source)
XLA Modules:
  0.0 724.9 jit_solution(14528736582536493586)
XLA Ops:
  14.5 4.9 collective-permute-start.1
  22.2 4.3 collective-permute-start.2
  29.5 6.1 collective-permute-start.3
  36.3 7.6 %all-to-all-start = ((s32[16,1,2]{2,1,0:T(1,128)}), s32[16,1,2]{2,1,0:T(1,128)S(1)}, u32[]{:S(2)}, u32[]{:S(2)}) async-start(s32[16,1,2]{2,1,0:T(1,128)} %copy.53), calls=%async_computation | async-start | bytes 16384 | tf_op jit(solution)/shard_map/all_to_all | solution.py:70
  45.0 8.8 %collective-permute-start.4 = (f32[16,32,256]{2,1,0:T(8,128)S(1)}, f32[16,32,256]{2,1,0:T(8,128)S(1)}, u32[]{:S(2)}, u32[]{:S(2)}) collective-permute-start(f32[16,32,256]{2,1,0:T(8,128)S(1)} %bitcast.131), channel_id=1, source_target_pairs={{0,256},{16,272},{32,288},{48,304},{64,320},{80,336},{96,352},{112... | collective-permute-start | bytes 1572872 | tf_op jit(solution)/shard_map/ppermute | solution.py:22
  53.9 18.4 %collective-permute-done.4 = f32[16,32,256]{2,1,0:T(8,128)S(1)} collective-permute-done((f32[16,32,256]{2,1,0:T(8,128)S(1)}, f32[16,32,256]{2,1,0:T(8,128)S(1)}, u32[]{:S(2)}, u32[]{:S(2)}) %collective-permute-start.4) | collective-permute-done | bytes 524320 | tf_op jit(solution)/shard_map/ppermute | solution.py:22
  73.1 4.1 gather_fusion.2
  79.0 235.3 %while.12 = (s32[]{:T(128)}, f32[32,128,128]{2,1,0:T(8,128)}, f32[8,4,256]{2,1,0:T(4,128)S(1)}, s32[8]{0:T(128)S(1)}, s32[32,1,9]{2,0,1:T(8,128)S(1)}, /*index=5...) while((s32[]{:T(128)}, f32[32,128,128]{2,1,0:T(8,128)}, ...), condition=%wide.region_3.4_spmd, body=%wide.region_0.3_spmd.sunk | while | flops 633674496 | bytes 35997664 | solution.py:115
  89.2 4.2 fusion.53
  93.4 3.5 reshape.317
  98.7 9.7 %scatter_fusion = f32[32,128,128]{2,1,0:T(8,128)} fusion(f32[32,128,128]{2,1,0:T(8,128)} %get-tuple-element.280, s32[36]{0:T(128)S(1)} %fusion.49, f32[36,128,128]{2,1,0:T(8,128)} %bitcast.126), kind=kCustom, calls=%fused_computation.3.clone.1 | custom fusion | flops 589824 | bytes 7078032 | tf_op jit(solution)/shard_map/while/body/eval_jaxpr/scatter-add | solution.py:111
  118.6 4.2 fusion.53
  128.1 9.7 %scatter_fusion = f32[32,128,128]{2,1,0:T(8,128)} fusion(f32[32,128,128]{2,1,0:T(8,128)} %get-tuple-element.280, s32[36]{0:T(128)S(1)} %fusion.49, f32[36,128,128]{2,1,0:T(8,128)} %bitcast.126), kind=kCustom, calls=%fused_computation.3.clone.1 | custom fusion | flops 589824 | bytes 7078032 | tf_op jit(solution)/shard_map/while/body/eval_jaxpr/scatter-add | solution.py:111
  148.0 4.2 fusion.53
  157.5 9.7 %scatter_fusion = f32[32,128,128]{2,1,0:T(8,128)} fusion(f32[32,128,128]{2,1,0:T(8,128)} %get-tuple-element.280, s32[36]{0:T(128)S(1)} %fusion.49, f32[36,128,128]{2,1,0:T(8,128)} %bitcast.126), kind=kCustom, calls=%fused_computation.3.clone.1 | custom fusion | flops 589824 | bytes 7078032 | tf_op jit(solution)/shard_map/while/body/eval_jaxpr/scatter-add | solution.py:111
  177.4 4.2 fusion.53
  181.6 3.5 reshape.317
  186.9 9.7 %scatter_fusion = f32[32,128,128]{2,1,0:T(8,128)} fusion(f32[32,128,128]{2,1,0:T(8,128)} %get-tuple-element.280, s32[36]{0:T(128)S(1)} %fusion.49, f32[36,128,128]{2,1,0:T(8,128)} %bitcast.126), kind=kCustom, calls=%fused_computation.3.clone.1 | custom fusion | flops 589824 | bytes 7078032 | tf_op jit(solution)/shard_map/while/body/eval_jaxpr/scatter-add | solution.py:111
  206.9 4.2 fusion.53
  211.0 3.5 reshape.317
  216.3 9.7 %scatter_fusion = f32[32,128,128]{2,1,0:T(8,128)} fusion(f32[32,128,128]{2,1,0:T(8,128)} %get-tuple-element.280, s32[36]{0:T(128)S(1)} %fusion.49, f32[36,128,128]{2,1,0:T(8,128)} %bitcast.126), kind=kCustom, calls=%fused_computation.3.clone.1 | custom fusion | flops 589824 | bytes 7078032 | tf_op jit(solution)/shard_map/while/body/eval_jaxpr/scatter-add | solution.py:111
  236.3 4.2 fusion.53
  245.8 9.7 %scatter_fusion = f32[32,128,128]{2,1,0:T(8,128)} fusion(f32[32,128,128]{2,1,0:T(8,128)} %get-tuple-element.280, s32[36]{0:T(128)S(1)} %fusion.49, f32[36,128,128]{2,1,0:T(8,128)} %bitcast.126), kind=kCustom, calls=%fused_computation.3.clone.1 | custom fusion | flops 589824 | bytes 7078032 | tf_op jit(solution)/shard_map/while/body/eval_jaxpr/scatter-add | solution.py:111
  265.7 4.2 fusion.53
  269.9 3.5 reshape.317
  275.2 9.7 %scatter_fusion = f32[32,128,128]{2,1,0:T(8,128)} fusion(f32[32,128,128]{2,1,0:T(8,128)} %get-tuple-element.280, s32[36]{0:T(128)S(1)} %fusion.49, f32[36,128,128]{2,1,0:T(8,128)} %bitcast.126), kind=kCustom, calls=%fused_computation.3.clone.1 | custom fusion | flops 589824 | bytes 7078032 | tf_op jit(solution)/shard_map/while/body/eval_jaxpr/scatter-add | solution.py:111
  295.1 4.2 fusion.53
  304.6 9.6 %scatter_fusion = f32[32,128,128]{2,1,0:T(8,128)} fusion(f32[32,128,128]{2,1,0:T(8,128)} %get-tuple-element.280, s32[36]{0:T(128)S(1)} %fusion.49, f32[36,128,128]{2,1,0:T(8,128)} %bitcast.126), kind=kCustom, calls=%fused_computation.3.clone.1 | custom fusion | flops 589824 | bytes 7078032 | tf_op jit(solution)/shard_map/while/body/eval_jaxpr/scatter-add | solution.py:111
  314.3 7.3 %all-to-all-start.1 = ((f32[16,2,128,128]{3,2,1,0:T(8,128)}), f32[16,2,128,128]{3,2,1,0:T(8,128)S(1)}, u32[]{:S(2)}, u32[]{:S(2)}) async-start(f32[16,2,128,128]{3,2,1,0:T(8,128)} %bitcast.128), calls=%async_computation.1 | async-start | bytes 4194304 | tf_op jit(solution)/shard_map/all_to_all | solution.py:117
  325.2 43.7 %all-to-all-done.1 = f32[16,2,128,128]{3,2,1,0:T(8,128)S(1)} async-done(((f32[16,2,128,128]{3,2,1,0:T(8,128)}), f32[16,2,128,128]{3,2,1,0:T(8,128)S(1)}, u32[]{:S(2)}, u32[]{:S(2)}) %all-to-all-start.1) | async-done | bytes 2097184 | tf_op jit(solution)/shard_map/all_to_all | solution.py:117
  372.7 180.6 %reduce-scatter.2.cloned.1.call-done = f32[32,256]{1,0:T(8,128)} async-done(((f32[1024,256]{1,0:T(8,128)}), f32[32,256]{1,0:T(8,128)}) %reduce-scatter.2.cloned.1.call-update) | async-done | bytes 32784 | tf_op jit(solution)/shard_map/reduce_scatter | solution.py:137
  554.7 161.4 %all-reduce.2.cloned.1.call-done = f32[16,128,128]{2,1,0:T(8,128)} async-done(((f32[16,128,128]{2,1,0:T(8,128)}), f32[16,128,128]{2,1,0:T(8,128)}) %all-reduce.2.cloned.1.call-update) | async-done | bytes 1048592 | tf_op jit(solution)/shard_map/psum | solution.py:129
  (284 shorter events, 132.8 us)
Async XLA Ops:
  7.2 28.4 %copy-start.4 = (s32[1,1,16,2]{2,3,1,0:T(2,128)S(1)}, s32[1,1,16,2]{2,3,1,0:T(2,128)}, u32[]{:S(2)}) copy-start(s32[1,1,16,2]{2,3,1,0:T(2,128)} %param.20) | copy-start | bytes 388
  7.2 36.9 %copy-start.3 = (s32[32,1,9]{0,1,2:T(1,128)S(1)}, s32[32,1,9]{0,1,2:T(1,128)}, u32[]{:S(2)}) copy-start(s32[32,1,9]{0,1,2:T(1,128)} %param.21) | copy-start | bytes 3460
  7.2 65.9 %all-gather.2.cloned.1.call-start = ((), (), s32[]{:S(2)}) async-start(), calls=%async_computation.3 | async-start | bytes 8912896 | tf_op jit(solution)/shard_map/all_gather | solution.py:74
  8.7 5.8 collective-permute-start
  14.5 7.7 %collective-permute-start.1 = (f32[2,32,256]{2,1,0:T(8,128)S(1)}, f32[2,32,256]{2,1,0:T(8,128)S(1)}, u32[]{:S(2)}, u32[]{:S(2)}) collective-permute-start(f32[2,32,256]{2,1,0:T(8,128)S(1)} %get-tuple-element.161), channel_id=1, source_target_pairs={{0,32},{16,48},{32,0},{48,16},{64,96},{80,112},{96,64},{112,80},{1... | collective-permute-start | bytes 196616 | tf_op jit(solution)/shard_map/ppermute | solution.py:22
  22.2 7.2 collective-permute-start.2
  29.5 15.5 %collective-permute-start.3 = (f32[8,32,256]{2,1,0:T(8,128)S(1)}, f32[8,32,256]{2,1,0:T(8,128)S(1)}, u32[]{:S(2)}, u32[]{:S(2)}) collective-permute-start(f32[8,32,256]{2,1,0:T(8,128)S(1)} %bitcast.137), channel_id=1, source_target_pairs={{0,128},{16,144},{32,160},{48,176},{64,192},{80,208},{96,224},{112... | collective-permute-start | bytes 786440 | tf_op jit(solution)/shard_map/ppermute | solution.py:22
  36.3 278.0 %all-to-all-start = ((s32[16,1,2]{2,1,0:T(1,128)}), s32[16,1,2]{2,1,0:T(1,128)S(1)}, u32[]{:S(2)}, u32[]{:S(2)}) async-start(s32[16,1,2]{2,1,0:T(1,128)} %copy.53), calls=%async_computation | async-start | bytes 16384 | tf_op jit(solution)/shard_map/all_to_all | solution.py:70
  45.0 27.2 %collective-permute-start.4 = (f32[16,32,256]{2,1,0:T(8,128)S(1)}, f32[16,32,256]{2,1,0:T(8,128)S(1)}, u32[]{:S(2)}, u32[]{:S(2)}) collective-permute-start(f32[16,32,256]{2,1,0:T(8,128)S(1)} %bitcast.131), channel_id=1, source_target_pairs={{0,256},{16,272},{32,288},{48,304},{64,320},{80,336},{96,352},{112... | collective-permute-start | bytes 1572872 | tf_op jit(solution)/shard_map/ppermute | solution.py:22
  79.0 3.8 copy-start
  98.7 9.7 %copy-start.1 = (bf16[32,128,128]{2,1,0:T(8,128)(2,1)S(1)}, bf16[32,128,128]{2,1,0:T(8,128)(2,1)}, u32[]{:S(2)}) copy-start(bf16[32,128,128]{2,1,0:T(8,128)(2,1)} %copy-done) | copy-start | bytes 3145732 | tf_op jit(solution)/shard_map/while
  108.4 3.8 copy-start
  128.1 9.7 %copy-start.1 = (bf16[32,128,128]{2,1,0:T(8,128)(2,1)S(1)}, bf16[32,128,128]{2,1,0:T(8,128)(2,1)}, u32[]{:S(2)}) copy-start(bf16[32,128,128]{2,1,0:T(8,128)(2,1)} %copy-done) | copy-start | bytes 3145732 | tf_op jit(solution)/shard_map/while
  137.8 3.8 copy-start
  157.5 9.7 %copy-start.1 = (bf16[32,128,128]{2,1,0:T(8,128)(2,1)S(1)}, bf16[32,128,128]{2,1,0:T(8,128)(2,1)}, u32[]{:S(2)}) copy-start(bf16[32,128,128]{2,1,0:T(8,128)(2,1)} %copy-done) | copy-start | bytes 3145732 | tf_op jit(solution)/shard_map/while
  167.2 3.8 copy-start
  186.9 9.7 %copy-start.1 = (bf16[32,128,128]{2,1,0:T(8,128)(2,1)S(1)}, bf16[32,128,128]{2,1,0:T(8,128)(2,1)}, u32[]{:S(2)}) copy-start(bf16[32,128,128]{2,1,0:T(8,128)(2,1)} %copy-done) | copy-start | bytes 3145732 | tf_op jit(solution)/shard_map/while
  196.6 3.8 copy-start
  216.3 9.8 %copy-start.1 = (bf16[32,128,128]{2,1,0:T(8,128)(2,1)S(1)}, bf16[32,128,128]{2,1,0:T(8,128)(2,1)}, u32[]{:S(2)}) copy-start(bf16[32,128,128]{2,1,0:T(8,128)(2,1)} %copy-done) | copy-start | bytes 3145732 | tf_op jit(solution)/shard_map/while
  226.1 3.8 copy-start
  245.8 9.7 %copy-start.1 = (bf16[32,128,128]{2,1,0:T(8,128)(2,1)S(1)}, bf16[32,128,128]{2,1,0:T(8,128)(2,1)}, u32[]{:S(2)}) copy-start(bf16[32,128,128]{2,1,0:T(8,128)(2,1)} %copy-done) | copy-start | bytes 3145732 | tf_op jit(solution)/shard_map/while
  255.5 3.8 copy-start
  275.2 9.7 %copy-start.1 = (bf16[32,128,128]{2,1,0:T(8,128)(2,1)S(1)}, bf16[32,128,128]{2,1,0:T(8,128)(2,1)}, u32[]{:S(2)}) copy-start(bf16[32,128,128]{2,1,0:T(8,128)(2,1)} %copy-done) | copy-start | bytes 3145732 | tf_op jit(solution)/shard_map/while
  284.9 3.8 copy-start
  304.6 9.6 %copy-start.1 = (bf16[32,128,128]{2,1,0:T(8,128)(2,1)S(1)}, bf16[32,128,128]{2,1,0:T(8,128)(2,1)}, u32[]{:S(2)}) copy-start(bf16[32,128,128]{2,1,0:T(8,128)(2,1)} %copy-done) | copy-start | bytes 3145732 | tf_op jit(solution)/shard_map/while
  314.3 54.7 %all-to-all-start.1 = ((f32[16,2,128,128]{3,2,1,0:T(8,128)}), f32[16,2,128,128]{3,2,1,0:T(8,128)S(1)}, u32[]{:S(2)}, u32[]{:S(2)}) async-start(f32[16,2,128,128]{3,2,1,0:T(8,128)} %bitcast.128), calls=%async_computation.1 | async-start | bytes 4194304 | tf_op jit(solution)/shard_map/all_to_all | solution.py:117
  321.5 231.7 %reduce-scatter.2.cloned.1.call-start = ((), (), s32[]{:S(2)}) async-start(), calls=%async_computation.5 | async-start | bytes 1081344 | tf_op jit(solution)/shard_map/reduce_scatter | solution.py:137
  323.9 392.2 %all-reduce.2.cloned.1.call-start = ((), (), s32[]{:S(2)}) async-start(), calls=%async_computation.4 | async-start | bytes 2097152 | tf_op jit(solution)/shard_map/psum | solution.py:129
  371.7 1.0 copy-start.2
Sparse Core Ops, SparseCore 0:
  10.1 61.5 all-gather.1
  326.8 226.4 reduce-scatter.1
  557.3 158.7 all-reduce.1
